TPU v7x, 32 devices: a whole 2x2x4 slice. The times are simulated.
32 devices in a mesh: member: 2 (over y), lat: 8 (over z, core), lon: 2 (over x).
Axes of the slice: x: 2, y: 2, z: 4, core: 2. Of those that a mesh axis runs over, the one named last changes fastest.
Arguments:
- state: bfloat16 [72, 64, 256], P(None, 'lat', 'lon'), may hold values from -6 to 6
- noise: bfloat16 [2, 2, 8, 64, 256], P('member', None, None, 'lat', 'lon'), may hold values from -6 to 6
- target: bfloat16 [2, 72, 64, 256], P(None, None, 'lat', 'lon'), may hold values from -6 to 6
- encoder_state_weight: bfloat16 [512, 72], replicated, may hold values from -0.75 to 0.75
- enc_noise: bfloat16 [512, 8], replicated, may hold values from -2 to 2
- lat_taps: float32 [4, 7, 512], replicated, may hold values from -1.75 to 1.75
- lon_taps: float32 [4, 6, 512], replicated, may hold values from -1.75 to 1.75
- gains: float32 [4, 512], replicated, may hold values from 0.25 to 1.75
- mix: bfloat16 [4, 512, 512], replicated, may hold values from -0.25 to 0.25
- decode: bfloat16 [72, 512], replicated, may hold values from -0.25 to 0.25
Outputs:
- trajectory_predictions: bfloat16 [2, 2, 72, 64, 256], P('member', None, None, 'lat', 'lon')
- probabilistic_error: float32 [72, 64, 256], P('member', 'lat', 'lon')
All inputs are finite; a program needn't handle non-finite values.
Results may differ from a plain program's by a relative error of at most 0.015.
Values may be sent and summed in bfloat16 or wider, within the bound.
A program may use at most 64 MiB of HBM per device.

v0:
```python
import functools

import jax
import jax.numpy as jnp
import numpy as np
from jax import lax
from jax.experimental import pallas as pl
from jax.experimental.pallas import tpu as pltpu
from jax.sharding import PartitionSpec as P

MESH = pl.DeviceIdType.MESH
epsilon = 1e-05
REACH = 3
CHUNK = 16


def edge_maps(rows, cols):
    edges = 2 * REACH
    fold = 2
    lanes = cols // fold
    assert rows * edges <= lanes
    take = np.zeros((fold, rows * cols, cols), np.float32)
    for half in range(fold):
        for row in range(rows):
            for k in range(edges):
                col = k if k < REACH else cols - edges + k
                take[half, row * cols + col, half * lanes + row * edges + k] = 1.0
    return take, take.transpose(0, 2, 1)


def rollout_kernel(
    count,
    layers,
    state,
    noise,
    taps,
    enc_state,
    enc_noise,
    mix,
    decode,
    take,
    give,
    trajectory,
    field,
    conv,
    edge,
    current,
    normed,
    sums,
    packed_out,
    packed_in,
    send_sem,
    recv_sem,
):
    rows, _, cols = state.shape
    channels = mix.shape[1]
    half = channels // 2
    steps = noise.shape[0]
    total_layers = steps * layers
    me = lax.axis_index("lat")
    peer = 1 - lax.axis_index("lon")
    has_up = me > 0
    has_down = me < count - 1

    zero = jnp.zeros((REACH, channels, cols), jnp.bfloat16)
    for slot in range(2):
        field[slot, 0:REACH] = zero
        field[slot, REACH + rows : 2 * REACH + rows] = zero
    current[...] = state[...]

    barrier = pltpu.get_barrier_semaphore()

    @pl.when(has_up)
    def _():
        pl.semaphore_signal(barrier, inc=1, device_id={"lat": me - 1}, device_id_type=MESH)

    @pl.when(has_down)
    def _():
        pl.semaphore_signal(barrier, inc=1, device_id={"lat": me + 1}, device_id_type=MESH)

    pl.semaphore_signal(barrier, inc=1, device_id={"lon": peer}, device_id_type=MESH)
    pl.semaphore_wait(barrier, 1 + has_up.astype(jnp.int32) + has_down.astype(jnp.int32))

    def copy_up(slot):
        return pltpu.make_async_remote_copy(
            src_ref=field.at[slot, pl.ds(REACH, REACH)],
            dst_ref=field.at[slot, pl.ds(REACH + rows, REACH)],
            send_sem=send_sem.at[slot, 0],
            recv_sem=recv_sem.at[slot, 0],
            device_id={"lat": me - 1},
            device_id_type=MESH,
        )

    def copy_down(slot):
        return pltpu.make_async_remote_copy(
            src_ref=field.at[slot, pl.ds(rows, REACH)],
            dst_ref=field.at[slot, pl.ds(0, REACH)],
            send_sem=send_sem.at[slot, 1],
            recv_sem=recv_sem.at[slot, 1],
            device_id={"lat": me + 1},
            device_id_type=MESH,
        )

    def copy_across(slot):
        return pltpu.make_async_remote_copy(
            src_ref=packed_out.at[slot],
            dst_ref=packed_in.at[slot],
            send_sem=send_sem.at[slot, 2],
            recv_sem=recv_sem.at[slot, 2],
            device_id={"lon": peer},
            device_id_type=MESH,
        )

    def start_lat(slot):
        @pl.when(has_up)
        def _():
            copy_up(slot).start()

        @pl.when(has_down)
        def _():
            copy_down(slot).start()

    def start_lon(slot):
        total = None
        for part in range(2):
            strip = jnp.concatenate(
                [field[slot, REACH + row, part * half : (part + 1) * half] for row in range(rows)],
                axis=1,
            )
            term = jnp.dot(strip, take[part], preferred_element_type=jnp.float32)
            total = term if total is None else total + term
        packed_out[slot] = total.astype(jnp.bfloat16)
        copy_across(slot).start()

    def finish(slot):
        @pl.when(has_up)
        def _():
            copy_up(slot).wait_send()
            copy_down(slot).wait_recv()

        @pl.when(has_down)
        def _():
            copy_down(slot).wait_send()
            copy_up(slot).wait_recv()

        copy_across(slot).wait()
        for part in range(2):
            wide = jnp.dot(
                packed_in[slot], give[part], preferred_element_type=jnp.float32
            ).astype(jnp.bfloat16)
            for row in range(rows):
                edge[row, part * half : (part + 1) * half] = wide[:, row * cols : (row + 1) * cols]

    def encode(step, slot):
        for row in range(rows):
            hidden = jnp.dot(
                enc_state[...], current[row], preferred_element_type=jnp.float32
            ) + jnp.dot(enc_noise[...], noise[step, row], preferred_element_type=jnp.float32)
            field[slot, REACH + row] = hidden.astype(jnp.bfloat16)

    def tap(layer, at, index):
        return jnp.broadcast_to(taps[layer, pl.ds(at, CHUNK), index : index + 1], (CHUNK, cols))

    def own_rows(layer, slot):
        @pl.loop(0, channels // CHUNK)
        def _(block):
            at = pl.multiple_of(block * CHUNK, CHUNK)
            weights = [tap(layer, at, d) for d in range(2 * REACH + 1)]
            totals = [None] * rows
            for source in range(rows):
                x = field[slot, REACH + source, pl.ds(at, CHUNK)].astype(jnp.float32)
                for row in range(max(0, source - REACH), min(rows, source + REACH + 1)):
                    term = weights[source - row + REACH] * x
                    totals[row] = term if totals[row] is None else totals[row] + term
            for row in range(rows):
                conv[row, pl.ds(at, CHUNK)] = totals[row]

    def edge_rows(layer, slot):
        sums[...] = jnp.zeros(sums.shape, jnp.float32)
        lane = lax.broadcasted_iota(jnp.int32, (CHUNK, cols), 1)

        @pl.loop(0, channels // CHUNK)
        def _(block):
            at = pl.multiple_of(block * CHUNK, CHUNK)
            weights = [tap(layer, at, d) for d in range(4 * REACH + 1)]
            for row in range(rows):
                total = conv[row, pl.ds(at, CHUNK)]
                for source in range(row - REACH, row + REACH + 1):
                    if source < 0 or source >= rows:
                        x = field[slot, REACH + source, pl.ds(at, CHUNK)].astype(jnp.float32)
                        total = total + weights[source - row + REACH] * x
                x = field[slot, REACH + row, pl.ds(at, CHUNK)].astype(jnp.float32)
                far = edge[row, pl.ds(at, CHUNK)].astype(jnp.float32)
                index = 2 * REACH + 1
                for d in range(-REACH, REACH + 1):
                    if d == 0:
                        continue
                    outside = lane >= cols + d if d < 0 else lane < d
                    moved = pltpu.roll(jnp.where(outside, far, x), (-d) % cols, 1)
                    total = total + weights[index] * moved
                    index += 1
                conv[row, pl.ds(at, CHUNK)] = total
                square = total * total
                sums[0, row] += total[0:8] + total[8:16]
                sums[1, row] += square[0:8] + square[8:16]

    def mix_pair(layer, slot, following, pair):
        for place, row in enumerate(pair):
            center = jnp.sum(sums[0, row], axis=0, keepdims=True) / channels
            second = jnp.sum(sums[1, row], axis=0, keepdims=True) / channels
            scale = lax.rsqrt(jnp.maximum(second - center * center, 0.0) + epsilon)
            gain = taps[layer, :, 4 * REACH + 1 : 4 * REACH + 2]
            normed[:, place * cols : (place + 1) * cols] = (
                (conv[row] - center) * scale * gain
            ).astype(jnp.bfloat16)

        @pl.loop(0, channels // 128)
        def _(block):
            at = pl.multiple_of(block * 128, 128)
            mixed = jnp.dot(
                mix[layer, pl.ds(at, 128)], normed[...], preferred_element_type=jnp.float32
            )
            bent = mixed * (0.7978845608028654 + 0.035677408136300125 * (mixed * mixed))
            half_mixed = 0.5 * mixed
            bump = half_mixed + half_mixed * jnp.tanh(bent)
            for place, row in enumerate(pair):
                held = field[slot, REACH + row, pl.ds(at, 128)].astype(jnp.float32)
                field[following, REACH + row, pl.ds(at, 128)] = (
                    held + bump[:, place * cols : (place + 1) * cols]
                ).astype(jnp.bfloat16)

    encode(0, 0)
    start_lat(0)
    start_lon(0)

    outer = list(range(REACH)) + list(range(rows - 1, rows - 1 - REACH, -1))
    inner = list(range(REACH, rows - REACH))

    def pairs(items):
        return [items[k : k + 2] for k in range(0, len(items), 2)]

    @pl.loop(0, total_layers)
    def _(index):
        slot = index % 2
        following = 1 - slot
        layer = index % layers
        step = index // layers
        last = layer == layers - 1
        own_rows(layer, slot)
        finish(slot)
        edge_rows(layer, slot)
        for pair in pairs(outer):
            mix_pair(layer, slot, following, pair)

        @pl.when(jnp.logical_not(last))
        def _():
            start_lat(following)

        for pair in pairs(inner):
            mix_pair(layer, slot, following, pair)

        @pl.when(last)
        def _():
            for row in range(rows):
                decoded = jnp.dot(
                    decode[...], field[following, REACH + row], preferred_element_type=jnp.float32
                )
                fresh = (current[row].astype(jnp.float32) + decoded).astype(jnp.bfloat16)
                current[row] = fresh
                trajectory[step, row] = fresh

            @pl.when(step < steps - 1)
            def _():
                encode(step + 1, following)
                start_lat(following)

        @pl.when(index < total_layers - 1)
        def _():
            start_lon(following)


def rollout(count, state, noise, encoder_state_weight, enc_noise, lat_taps, lon_taps, gains, mix, decode):
    quantities, rows, cols = state.shape
    steps = noise.shape[1]
    layers, channels, _ = mix.shape
    take, give = edge_maps(rows, cols)
    table = jnp.concatenate([lat_taps, lon_taps, gains[:, None]], axis=1).transpose(0, 2, 1)
    vmem = pl.BlockSpec(memory_space=pltpu.VMEM)
    return pl.pallas_call(
        functools.partial(rollout_kernel, count, layers),
        out_shape=jax.ShapeDtypeStruct((steps, rows, quantities, cols), jnp.bfloat16),
        in_specs=[vmem] * 9,
        out_specs=vmem,
        scratch_shapes=[
            pltpu.VMEM((2, rows + 2 * REACH, channels, cols), jnp.bfloat16),
            pltpu.VMEM((rows, channels, cols), jnp.float32),
            pltpu.VMEM((rows, channels, cols), jnp.bfloat16),
            pltpu.VMEM((rows, quantities, cols), jnp.bfloat16),
            pltpu.VMEM((channels, 2 * cols), jnp.bfloat16),
            pltpu.VMEM((2, rows, 8, cols), jnp.float32),
            pltpu.VMEM((2, channels // 2, cols), jnp.bfloat16),
            pltpu.VMEM((2, channels // 2, cols), jnp.bfloat16),
            pltpu.SemaphoreType.DMA((2, 3)),
            pltpu.SemaphoreType.DMA((2, 3)),
        ],
        compiler_params=pltpu.CompilerParams(
            collective_id=0, has_side_effects=True, vmem_limit_bytes=40 * 1024 * 1024
        ),
    )(
        state.transpose(1, 0, 2),
        noise[0].transpose(0, 2, 1, 3),
        table,
        encoder_state_weight,
        enc_noise,
        mix,
        decode,
        jnp.asarray(take, jnp.bfloat16),
        jnp.asarray(give, jnp.bfloat16),
    )


def local(
    count, state, noise, target, encoder_state_weight, enc_noise, lat_taps, lon_taps, gains, mix, decode
):
    quantity_total = state.shape[0]
    forecast = rollout(
        count, state, noise, encoder_state_weight, enc_noise, lat_taps, lon_taps, gains, mix, decode
    )
    trajectory_predictions = forecast.transpose(0, 2, 1, 3)[None]
    members = lax.axis_size("member")
    scale = float(members)
    regrouped = lax.all_to_all(
        trajectory_predictions, "member", split_axis=2, concat_axis=0, tiled=True
    )
    quantities_real = regrouped.astype(jnp.float32)
    block = quantity_total // members
    start = lax.axis_index("member") * block
    target_block = lax.dynamic_slice_in_dim(target, start, block, 1).astype(jnp.float32)
    skill = jnp.sum(jnp.abs(quantities_real - target_block[None]), axis=(0, 1))
    spread = jnp.zeros(skill.shape, jnp.float32)
    for other in range(members):
        spread = spread + jnp.sum(jnp.abs(quantities_real - quantities_real[other][None]), axis=(0, 1))
    probabilistic_error = skill / scale - spread / (2.0 * scale * (scale - 1.0))
    return (trajectory_predictions, probabilistic_error)


def solution(mesh):
    assert mesh.shape["lon"] == 2
    in_specs = (
        P(None, "lat", "lon"),
        P("member", None, None, "lat", "lon"),
        P(None, None, "lat", "lon"),
        P(),
        P(),
        P(),
        P(),
        P(),
        P(),
        P(),
    )
    out_specs = (P("member", None, None, "lat", "lon"), P("member", "lat", "lon"))
    return jax.shard_map(
        functools.partial(local, mesh.shape["lat"]),
        mesh=mesh,
        in_specs=in_specs,
        out_specs=out_specs,
        check_vma=False,
    )
```

profile of v0, /device:TPU:16, one launch (start us, length us, event | category | flops | bytes accessed | tf_op | source)
XLA Modules:
  0.0 152.6 jit_solution(10267407513697095622)
XLA Ops:
  0.6 0.0 copy-start
  0.6 1.7 %copy.41 = bf16[72,8,128]{2,0,1:T(8,128)(2,1)} copy(bf16[72,8,128]{2,1,0:T(8,128)(2,1)} %param.12) | data formatting | bytes 294912 | tf_op args[0]
  2.4 0.8 copy.42
  3.1 0.9 pad_maximum_fusion
  4.0 0.4 copy.33
  4.4 1.6 %copy.34.enc_state = bf16[512,72]{1,0:T(8,128)(2,1)} copy(bf16[512,72]{0,1:T(8,128)(2,1)} %param.15) | data formatting | bytes 147456 | tf_op args[3]
  6.1 1.5 copy.35.enc_noise
  7.5 0.0 copy-done
  7.5 0.0 copy-start.1
  7.5 0.9 copy-done.1
  8.4 0.0 copy-start.2
  8.4 1.0 copy-done.2
  9.5 0.0 copy-start.3
  9.5 1.0 copy-done.3
  10.5 0.0 copy-start.4
  10.5 0.9 copy-done.4
  11.4 0.0 copy-start.5
  11.4 0.9 copy-done.5
  12.3 0.0 copy-start.6
  12.3 0.9 copy-done.6
  13.2 128.0 %shard_map.131 = bf16[2,8,72,128]{3,2,1,0:T(8,128)(2,1)S(1)} custom-call(bf16[8,72,128]{2,1,0:T(8,128)(2,1)S(1)} %bitcast.45, bf16[2,8,8,128]{3,2,1,0:T(8,128)(2,1)S(1)} %bitcast.46, f32[4,512,14]{2,1,0:T(8,128)S(1)} %bitcast.42, bf16[512,72]{1,0:T(8,128)(2,1)S(1)} %copy-done.4, bf16[512,8]{1,0:T(8,128)(2,1)S(1)} %copy-done.5, ...), custom_call_target="tpu_custom_call" | custom-call | tf_op jit(solution)/shard_map/pallas_call | solution.py:289
  141.3 0.7 copy.36
  142.0 3.4 %all-to-all-start = ((bf16[1,2,72,8,128]{4,3,1,0,2:T(8,128)(2,1)}), bf16[1,2,72,8,128]{4,3,1,0,2:T(8,128)(2,1)S(1)}, u32[]{:S(2)}, u32[]{:S(2)}) async-start(bf16[1,2,72,8,128]{4,3,1,0,2:T(8,128)(2,1)} %copy.36), calls=%async_computation | async-start | bytes 589824 | tf_op jit(solution)/shard_map/all_to_all | solution.py:332
  145.5 0.8 copy.38
  146.2 0.9 dynamic-slice_convert_fusion
  147.1 4.4 %all-to-all-done = bf16[1,2,72,8,128]{4,3,1,0,2:T(8,128)(2,1)S(1)} async-done(((bf16[1,2,72,8,128]{4,3,1,0,2:T(8,128)(2,1)}), bf16[1,2,72,8,128]{4,3,1,0,2:T(8,128)(2,1)S(1)}, u32[]{:S(2)}, u32[]{:S(2)}) %all-to-all-start) | async-done | bytes 294944 | tf_op jit(solution)/shard_map/all_to_all | solution.py:332
  151.7 0.2 fusion.4
  151.9 0.7 multiply_subtract_fusion
  (3 shorter events, 0.1 us)
Async XLA Ops:
  0.6 6.9 %copy-start = (bf16[4,512,512]{2,1,0:T(8,128)(2,1)S(1)}, bf16[4,512,512]{2,1,0:T(8,128)(2,1)}, u32[]{:S(2)}) copy-start(bf16[4,512,512]{2,1,0:T(8,128)(2,1)} %mix.1) | copy-start | bytes 6291460
  7.5 0.9 copy-start.1
  8.4 1.0 copy-start.2
  9.5 1.0 copy-start.3
  10.5 0.9 copy-start.4
  11.4 0.9 copy-start.5
  12.3 0.9 copy-start.6
  142.0 9.6 %all-to-all-start = ((bf16[1,2,72,8,128]{4,3,1,0,2:T(8,128)(2,1)}), bf16[1,2,72,8,128]{4,3,1,0,2:T(8,128)(2,1)S(1)}, u32[]{:S(2)}, u32[]{:S(2)}) async-start(bf16[1,2,72,8,128]{4,3,1,0,2:T(8,128)(2,1)} %copy.36), calls=%async_computation | async-start | bytes 589824 | tf_op jit(solution)/shard_map/all_to_all | solution.py:332
where the time goes:
time: 153 us
  Pallas kernels  128 us (84%)
  local copies, waits for them, and re-layouts  13.2 us (9%)
  waiting for transfers between devices  4.41 us (3%)
  starting transfers between devices  3.45 us (2%)
  other arithmetic  2.77 us (2%)
    pallas_call x1, Pallas kernels, rollout(): pl.pallas_call(functools.partial(rollout_kernel, count, layers), out_shap...  128 us
    unnamed x19, local copies, waits for them, and re-layouts  12.1 us
    all_to_all x1, waiting for transfers between devices, local(): lax.all_to_all(trajectory_predictions, 'member', split_axis=2, concat_axi...  4.41 us
    all_to_all x1, starting transfers between devices, local(): lax.all_to_all(trajectory_predictions, 'member', split_axis=2, concat_axi...  3.45 us
  transfers between devices with their start and end apart: 1, of which 1 were waited for; matrix products, arithmetic and copies ran while one was open for 1% of the time, Pallas kernels for 0%

commit v1 on v0

--- a/solution.py
+++ b/solution.py
@@ -183,25 +183,27 @@
         def _(block):
             at = pl.multiple_of(block * CHUNK, CHUNK)
             weights = [tap(layer, at, d) for d in range(4 * REACH + 1)]
-            for row in range(rows):
-                total = conv[row, pl.ds(at, CHUNK)]
+            near = [field[slot, k, pl.ds(at, CHUNK)] for k in range(rows + 2 * REACH)]
+            far = [edge[row, pl.ds(at, CHUNK)] for row in range(rows)]
+            totals = [conv[row, pl.ds(at, CHUNK)] for row in range(rows)]
+            for row in range(rows):
                 for source in range(row - REACH, row + REACH + 1):
                     if source < 0 or source >= rows:
-                        x = field[slot, REACH + source, pl.ds(at, CHUNK)].astype(jnp.float32)
-                        total = total + weights[source - row + REACH] * x
-                x = field[slot, REACH + row, pl.ds(at, CHUNK)].astype(jnp.float32)
-                far = edge[row, pl.ds(at, CHUNK)].astype(jnp.float32)
-                index = 2 * REACH + 1
-                for d in range(-REACH, REACH + 1):
-                    if d == 0:
-                        continue
-                    outside = lane >= cols + d if d < 0 else lane < d
-                    moved = pltpu.roll(jnp.where(outside, far, x), (-d) % cols, 1)
-                    total = total + weights[index] * moved
-                    index += 1
-                conv[row, pl.ds(at, CHUNK)] = total
-                square = total * total
-                sums[0, row] += total[0:8] + total[8:16]
+                        x = near[REACH + source].astype(jnp.float32)
+                        totals[row] = totals[row] + weights[source - row + REACH] * x
+            index = 2 * REACH + 1
+            for d in range(-REACH, REACH + 1):
+                if d == 0:
+                    continue
+                outside = lane >= cols + d if d < 0 else lane < d
+                for row in range(rows):
+                    source = jnp.where(outside, far[row], near[REACH + row])
+                    totals[row] = totals[row] + weights[index] * pltpu.roll(source, (-d) % cols, 1).astype(jnp.float32)
+                index += 1
+            for row in range(rows):
+                square = totals[row] * totals[row]
+                conv[row, pl.ds(at, CHUNK)] = totals[row]
+                sums[0, row] += totals[row][0:8] + totals[row][8:16]
                 sums[1, row] += square[0:8] + square[8:16]
 
     def mix_pair(layer, slot, following, pair):
@@ -214,20 +216,15 @@
                 (conv[row] - center) * scale * gain
             ).astype(jnp.bfloat16)
 
-        @pl.loop(0, channels // 128)
-        def _(block):
-            at = pl.multiple_of(block * 128, 128)
-            mixed = jnp.dot(
-                mix[layer, pl.ds(at, 128)], normed[...], preferred_element_type=jnp.float32
-            )
-            bent = mixed * (0.7978845608028654 + 0.035677408136300125 * (mixed * mixed))
-            half_mixed = 0.5 * mixed
-            bump = half_mixed + half_mixed * jnp.tanh(bent)
-            for place, row in enumerate(pair):
-                held = field[slot, REACH + row, pl.ds(at, 128)].astype(jnp.float32)
-                field[following, REACH + row, pl.ds(at, 128)] = (
-                    held + bump[:, place * cols : (place + 1) * cols]
-                ).astype(jnp.bfloat16)
+        mixed = jnp.dot(mix[layer], normed[...], preferred_element_type=jnp.float32)
+        bent = mixed * (0.7978845608028654 + 0.035677408136300125 * (mixed * mixed))
+        half_mixed = 0.5 * mixed
+        bump = half_mixed + half_mixed * jnp.tanh(bent)
+        held = [field[slot, REACH + row].astype(jnp.float32) for row in pair]
+        for place, row in enumerate(pair):
+            field[following, REACH + row] = (
+                held[place] + bump[:, place * cols : (place + 1) * cols]
+            ).astype(jnp.bfloat16)
 
     encode(0, 0)
     start_lat(0)

time: 153 us -> 135 us (0.88)
  Pallas kernels: 128 us -> 110 us
    pallas_call x1, Pallas kernels: 128 us -> 110 us  [rollout(): pl.pallas_call(functools.partial(rollout_kernel, count, layers), out_shap...]
where the time goes in v1:
time: 135 us
  Pallas kernels  110 us (81%)
  local copies, waits for them, and re-layouts  13.2 us (10%)
  waiting for transfers between devices  4.44 us (3%)
  starting transfers between devices  3.45 us (3%)
  other arithmetic  2.77 us (2%)
    pallas_call x1, Pallas kernels, rollout(): pl.pallas_call(functools.partial(rollout_kernel, count, layers), out_shap...  110 us
    unnamed x19, local copies, waits for them, and re-layouts  12.1 us
    all_to_all x1, waiting for transfers between devices, local(): lax.all_to_all(trajectory_predictions, 'member', split_axis=2, concat_axi...  4.44 us
    all_to_all x1, starting transfers between devices, local(): lax.all_to_all(trajectory_predictions, 'member', split_axis=2, concat_axi...  3.45 us
  transfers between devices with their start and end apart: 1, of which 1 were waited for; matrix products, arithmetic and copies ran while one was open for 1% of the time, Pallas kernels for 0%

profile of v1, /device:TPU:16, one launch (start us, length us, event | category | flops | bytes accessed | tf_op | source)
XLA Modules:
  0.0 134.9 jit_solution(3917488199455063196)
XLA Ops:
  0.6 0.0 copy-start
  0.6 1.7 %copy.41 = bf16[72,8,128]{2,0,1:T(8,128)(2,1)} copy(bf16[72,8,128]{2,1,0:T(8,128)(2,1)} %param.12) | data formatting | bytes 294912 | tf_op args[0]
  2.4 0.8 copy.42
  3.1 0.9 pad_maximum_fusion
  4.0 0.4 copy.33
  4.4 1.6 %copy.34.enc_state = bf16[512,72]{1,0:T(8,128)(2,1)} copy(bf16[512,72]{0,1:T(8,128)(2,1)} %param.15) | data formatting | bytes 147456 | tf_op args[3]
  6.1 1.5 %copy.35.enc_noise = bf16[512,8]{1,0:T(8,128)(2,1)} copy(bf16[512,8]{0,1:T(8,128)(2,1)} %param.16) | data formatting | bytes 16384 | tf_op args[4]
  7.5 0.0 copy-done
  7.5 0.0 copy-start.1
  7.5 0.9 copy-done.1
  8.4 0.0 copy-start.2
  8.4 1.0 copy-done.2
  9.5 0.0 copy-start.3
  9.5 1.0 copy-done.3
  10.5 0.0 copy-start.4
  10.5 0.9 copy-done.4
  11.4 0.0 copy-start.5
  11.4 0.9 copy-done.5
  12.3 0.0 copy-start.6
  12.3 0.9 copy-done.6
  13.2 110.3 %shard_map.131 = bf16[2,8,72,128]{3,2,1,0:T(8,128)(2,1)S(1)} custom-call(bf16[8,72,128]{2,1,0:T(8,128)(2,1)S(1)} %bitcast.45, bf16[2,8,8,128]{3,2,1,0:T(8,128)(2,1)S(1)} %bitcast.46, f32[4,512,14]{2,1,0:T(8,128)S(1)} %bitcast.42, bf16[512,72]{1,0:T(8,128)(2,1)S(1)} %copy-done.4, bf16[512,8]{1,0:T(8,128)(2,1)S(1)} %copy-done.5, ...), custom_call_target="tpu_custom_call" | custom-call | tf_op jit(solution)/shard_map/pallas_call | solution.py:286
  123.5 0.7 copy.36
  124.2 3.4 %all-to-all-start = ((bf16[1,2,72,8,128]{4,3,1,0,2:T(8,128)(2,1)}), bf16[1,2,72,8,128]{4,3,1,0,2:T(8,128)(2,1)S(1)}, u32[]{:S(2)}, u32[]{:S(2)}) async-start(bf16[1,2,72,8,128]{4,3,1,0,2:T(8,128)(2,1)} %copy.36), calls=%async_computation | async-start | bytes 589824 | tf_op jit(solution)/shard_map/all_to_all | solution.py:329
  127.7 0.8 copy.38
  128.5 0.9 dynamic-slice_convert_fusion
  129.4 4.4 %all-to-all-done = bf16[1,2,72,8,128]{4,3,1,0,2:T(8,128)(2,1)S(1)} async-done(((bf16[1,2,72,8,128]{4,3,1,0,2:T(8,128)(2,1)}), bf16[1,2,72,8,128]{4,3,1,0,2:T(8,128)(2,1)S(1)}, u32[]{:S(2)}, u32[]{:S(2)}) %all-to-all-start) | async-done | bytes 294944 | tf_op jit(solution)/shard_map/all_to_all | solution.py:329
  134.0 0.2 fusion.4
  134.2 0.7 multiply_subtract_fusion
  (3 shorter events, 0.1 us)
Async XLA Ops:
  0.6 6.9 %copy-start = (bf16[4,512,512]{2,1,0:T(8,128)(2,1)S(1)}, bf16[4,512,512]{2,1,0:T(8,128)(2,1)}, u32[]{:S(2)}) copy-start(bf16[4,512,512]{2,1,0:T(8,128)(2,1)} %mix.1) | copy-start | bytes 6291460
  7.5 0.9 copy-start.1
  8.4 1.0 copy-start.2
  9.5 1.0 copy-start.3
  10.5 0.9 copy-start.4
  11.4 0.9 copy-start.5
  12.3 0.9 copy-start.6
  124.2 9.6 %all-to-all-start = ((bf16[1,2,72,8,128]{4,3,1,0,2:T(8,128)(2,1)}), bf16[1,2,72,8,128]{4,3,1,0,2:T(8,128)(2,1)S(1)}, u32[]{:S(2)}, u32[]{:S(2)}) async-start(bf16[1,2,72,8,128]{4,3,1,0,2:T(8,128)(2,1)} %copy.36), calls=%async_computation | async-start | bytes 589824 | tf_op jit(solution)/shard_map/all_to_all | solution.py:329

commit v2 on v1

--- a/solution.py
+++ b/solution.py
@@ -159,7 +159,8 @@
             field[slot, REACH + row] = hidden.astype(jnp.bfloat16)
 
     def tap(layer, at, index):
-        return jnp.broadcast_to(taps[layer, pl.ds(at, CHUNK), index : index + 1], (CHUNK, cols))
+        column = taps[layer, pl.ds(at, CHUNK), index : index + 1]
+        return jnp.broadcast_to(column, (CHUNK, cols)).astype(jnp.bfloat16)
 
     def own_rows(layer, slot):
         @pl.loop(0, channels // CHUNK)
@@ -168,12 +169,12 @@
             weights = [tap(layer, at, d) for d in range(2 * REACH + 1)]
             totals = [None] * rows
             for source in range(rows):
-                x = field[slot, REACH + source, pl.ds(at, CHUNK)].astype(jnp.float32)
+                x = field[slot, REACH + source, pl.ds(at, CHUNK)]
                 for row in range(max(0, source - REACH), min(rows, source + REACH + 1)):
                     term = weights[source - row + REACH] * x
                     totals[row] = term if totals[row] is None else totals[row] + term
             for row in range(rows):
-                conv[row, pl.ds(at, CHUNK)] = totals[row]
+                conv[row, pl.ds(at, CHUNK)] = totals[row].astype(jnp.float32)
 
     def edge_rows(layer, slot):
         sums[...] = jnp.zeros(sums.shape, jnp.float32)
@@ -185,11 +186,12 @@
             weights = [tap(layer, at, d) for d in range(4 * REACH + 1)]
             near = [field[slot, k, pl.ds(at, CHUNK)] for k in range(rows + 2 * REACH)]
             far = [edge[row, pl.ds(at, CHUNK)] for row in range(rows)]
-            totals = [conv[row, pl.ds(at, CHUNK)] for row in range(rows)]
+            held = [conv[row, pl.ds(at, CHUNK)] for row in range(rows)]
+            totals = [jnp.zeros((CHUNK, cols), jnp.bfloat16)] * rows
             for row in range(rows):
                 for source in range(row - REACH, row + REACH + 1):
                     if source < 0 or source >= rows:
-                        x = near[REACH + source].astype(jnp.float32)
+                        x = near[REACH + source]
                         totals[row] = totals[row] + weights[source - row + REACH] * x
             index = 2 * REACH + 1
             for d in range(-REACH, REACH + 1):
@@ -198,12 +200,13 @@
                 outside = lane >= cols + d if d < 0 else lane < d
                 for row in range(rows):
                     source = jnp.where(outside, far[row], near[REACH + row])
-                    totals[row] = totals[row] + weights[index] * pltpu.roll(source, (-d) % cols, 1).astype(jnp.float32)
+                    totals[row] = totals[row] + weights[index] * pltpu.roll(source, (-d) % cols, 1)
                 index += 1
             for row in range(rows):
-                square = totals[row] * totals[row]
-                conv[row, pl.ds(at, CHUNK)] = totals[row]
-                sums[0, row] += totals[row][0:8] + totals[row][8:16]
+                total = held[row] + totals[row].astype(jnp.float32)
+                square = total * total
+                conv[row, pl.ds(at, CHUNK)] = total
+                sums[0, row] += total[0:8] + total[8:16]
                 sums[1, row] += square[0:8] + square[8:16]
 
     def mix_pair(layer, slot, following, pair):

time: 135 us -> 132 us (0.978)
  Pallas kernels: 110 us -> 107 us
    pallas_call x1, Pallas kernels: 110 us -> 107 us  [rollout(): pl.pallas_call(functools.partial(rollout_kernel, count, layers), out_shap...]
where the time goes in v2:
time: 132 us; the launch traced here: 131 us
  Pallas kernels  107 us (81%)
  local copies, waits for them, and re-layouts  13.2 us (10%)
  waiting for transfers between devices  4.44 us (3%)
  starting transfers between devices  3.45 us (3%)
  other arithmetic  2.77 us (2%)
    pallas_call x1, Pallas kernels, rollout(): pl.pallas_call(functools.partial(rollout_kernel, count, layers), out_shap...  107 us
    unnamed x19, local copies, waits for them, and re-layouts  12.1 us
    all_to_all x1, waiting for transfers between devices, local(): lax.all_to_all(trajectory_predictions, 'member', split_axis=2, concat_axi...  4.44 us
    all_to_all x1, starting transfers between devices, local(): lax.all_to_all(trajectory_predictions, 'member', split_axis=2, concat_axi...  3.45 us
  transfers between devices with their start and end apart: 1, of which 1 were waited for; matrix products, arithmetic and copies ran while one was open for 1% of the time, Pallas kernels for 0%

profile of v2, /device:TPU:16, one launch (start us, length us, event | category | flops | bytes accessed | tf_op | source)
XLA Modules:
  0.0 131.2 jit_solution(12284922379460682193)
XLA Ops:
  0.6 0.0 copy-start
  0.6 1.7 %copy.41 = bf16[72,8,128]{2,0,1:T(8,128)(2,1)} copy(bf16[72,8,128]{2,1,0:T(8,128)(2,1)} %param.12) | data formatting | bytes 294912 | tf_op args[0]
  2.4 0.8 copy.42
  3.1 0.9 pad_maximum_fusion
  4.0 0.4 copy.33
  4.4 1.6 %copy.34.enc_state = bf16[512,72]{1,0:T(8,128)(2,1)} copy(bf16[512,72]{0,1:T(8,128)(2,1)} %param.15) | data formatting | bytes 147456 | tf_op args[3]
  6.1 1.5 %copy.35.enc_noise = bf16[512,8]{1,0:T(8,128)(2,1)} copy(bf16[512,8]{0,1:T(8,128)(2,1)} %param.16) | data formatting | bytes 16384 | tf_op args[4]
  7.5 0.0 copy-done
  7.5 0.0 copy-start.1
  7.5 0.9 copy-done.1
  8.4 0.0 copy-start.2
  8.4 1.0 copy-done.2
  9.5 0.0 copy-start.3
  9.5 1.0 copy-done.3
  10.5 0.0 copy-start.4
  10.5 0.9 copy-done.4
  11.4 0.0 copy-start.5
  11.4 0.9 copy-done.5
  12.3 0.0 copy-start.6
  12.3 0.9 copy-done.6
  13.2 106.6 %shard_map.131 = bf16[2,8,72,128]{3,2,1,0:T(8,128)(2,1)S(1)} custom-call(bf16[8,72,128]{2,1,0:T(8,128)(2,1)S(1)} %bitcast.45, bf16[2,8,8,128]{3,2,1,0:T(8,128)(2,1)S(1)} %bitcast.46, f32[4,512,14]{2,1,0:T(8,128)S(1)} %bitcast.42, bf16[512,72]{1,0:T(8,128)(2,1)S(1)} %copy-done.4, bf16[512,8]{1,0:T(8,128)(2,1)S(1)} %copy-done.5, ...), custom_call_target="tpu_custom_call" | custom-call | tf_op jit(solution)/shard_map/pallas_call | solution.py:289
  119.8 0.7 copy.36
  120.5 3.4 %all-to-all-start = ((bf16[1,2,72,8,128]{4,3,1,0,2:T(8,128)(2,1)}), bf16[1,2,72,8,128]{4,3,1,0,2:T(8,128)(2,1)S(1)}, u32[]{:S(2)}, u32[]{:S(2)}) async-start(bf16[1,2,72,8,128]{4,3,1,0,2:T(8,128)(2,1)} %copy.36), calls=%async_computation | async-start | bytes 589824 | tf_op jit(solution)/shard_map/all_to_all | solution.py:332
  124.0 0.8 copy.38
  124.8 0.9 dynamic-slice_convert_fusion
  125.7 4.4 %all-to-all-done = bf16[1,2,72,8,128]{4,3,1,0,2:T(8,128)(2,1)S(1)} async-done(((bf16[1,2,72,8,128]{4,3,1,0,2:T(8,128)(2,1)}), bf16[1,2,72,8,128]{4,3,1,0,2:T(8,128)(2,1)S(1)}, u32[]{:S(2)}, u32[]{:S(2)}) %all-to-all-start) | async-done | bytes 294944 | tf_op jit(solution)/shard_map/all_to_all | solution.py:332
  130.2 0.2 fusion.4
  130.5 0.7 multiply_subtract_fusion
  (3 shorter events, 0.1 us)
Async XLA Ops:
  0.6 6.9 %copy-start = (bf16[4,512,512]{2,1,0:T(8,128)(2,1)S(1)}, bf16[4,512,512]{2,1,0:T(8,128)(2,1)}, u32[]{:S(2)}) copy-start(bf16[4,512,512]{2,1,0:T(8,128)(2,1)} %mix.1) | copy-start | bytes 6291460
  7.5 0.9 copy-start.1
  8.4 1.0 copy-start.2
  9.5 1.0 copy-start.3
  10.5 0.9 copy-start.4
  11.4 0.9 copy-start.5
  12.3 0.9 copy-start.6
  120.5 9.6 %all-to-all-start = ((bf16[1,2,72,8,128]{4,3,1,0,2:T(8,128)(2,1)}), bf16[1,2,72,8,128]{4,3,1,0,2:T(8,128)(2,1)S(1)}, u32[]{:S(2)}, u32[]{:S(2)}) async-start(bf16[1,2,72,8,128]{4,3,1,0,2:T(8,128)(2,1)} %copy.36), calls=%async_computation | async-start | bytes 589824 | tf_op jit(solution)/shard_map/all_to_all | solution.py:332
